TPU v7x, 256 devices: a whole 4x4x8 slice. The times are simulated.
256 devices in a mesh: seq: 32 (over y, z), store: 8 (over x, core).
Axes of the slice: x: 4, y: 4, z: 8, core: 2. Of those that a mesh axis runs over, the one named last changes fastest.
Arguments:
- hidden: bfloat16 [24576, 4096], P('seq', 'store'), may hold values from -6 to 6
- nbr_shard: int32 [384, 2], P('seq'), may hold values from 0 to 31, all different within a row; in each aligned block of 12 rows (0 to 11, 12 to 23, ...) at most 2 rows name the same one
- nbr_block: int32 [384, 2], P('seq'), may hold values from 0 to 7
- seq_lengths: int32 [24], replicated, may hold values from 1 to 128, 384 in all
- kv_store: bfloat16 [256, 128, 2, 4096], P('seq', None, None, 'store'), may hold values from -250 to 250
- w_query: bfloat16 [4096, 4096], P(None, 'store'), may hold values from -0.09375 to 0.09375
- w_out: bfloat16 [4096, 4096], P('store'), may hold values from -0.125 to 0.125
Outputs:
- output: bfloat16 [24576, 4096], P('seq', 'store')
Inputs may be any that keep to these rules, and one draw needn't show every extreme that they name: `nbr_shard`: among the spans of one device, no store shard is named by more than 2 neighbour entries; the 2 neighbours of a span lie on different shards. `seq_lengths`: the lengths sum to 384; the longest is 128.
All inputs are finite; a program needn't handle non-finite values.
Results may differ from a plain program's by a relative error of at most 0.025.
Values may be sent and summed in bfloat16 or wider, within the bound.
No kernel may reach another device: no remote copies, remote signals or barrier semaphores. Data moves between devices by JAX's collectives and lax.ppermute only.
A program may use at most 128 MiB of HBM per device.

v0:
```python
import jax
import jax.numpy as jnp
from jax import lax
from jax.sharding import PartitionSpec as P

HEAD_DIM = 128
SPAN = 64
NBR = 2
NBR_LEN = 128


def shifted(array, axis, by):
    size = lax.axis_size(axis)
    pairs = [(i, i + by) for i in range(size) if 0 <= i + by < size]
    return lax.ppermute(array, axis, pairs)


def partial_attention(queries, blocks):
    width = queries.shape[-1]
    head_count = width // HEAD_DIM
    query_heads = queries.reshape(queries.shape[:-1] + (head_count, HEAD_DIM))
    key_heads = blocks[..., :width].reshape(blocks.shape[:-1] + (head_count, HEAD_DIM))
    value_heads = blocks[..., width:].reshape(blocks.shape[:-1] + (head_count, HEAD_DIM))
    scores = jnp.einsum(
        "...qhd,...khd->...hqk", query_heads, key_heads, preferred_element_type=jnp.float32
    ) * HEAD_DIM ** (-0.5)
    peaks = jnp.max(scores, axis=-1)
    weights = jnp.exp(scores - peaks[..., None])
    totals = jnp.sum(weights, axis=-1)
    rounded = weights.astype(jnp.bfloat16)
    mixed = jnp.einsum(
        "...hqk,...khd->...hqd", rounded, value_heads, preferred_element_type=jnp.float32
    ).astype(jnp.bfloat16)
    return (mixed, peaks, totals)


def combine(mixed, peaks, totals, axis_pos):
    best = jnp.max(peaks, axis=axis_pos, keepdims=True)
    factors = jnp.exp(peaks - best)
    numer = jnp.sum(factors[..., None] * mixed.astype(jnp.float32), axis=axis_pos)
    denom = jnp.sum(factors * totals, axis=axis_pos)
    return numer / denom[..., None]


def on_device(hidden, nbr_shard, nbr_block, seq_lengths, kv_store, w_query, w_out):
    row_count = hidden.shape[0]
    span_count = row_count // SPAN
    width = w_query.shape[1]
    peers = lax.axis_size("seq")
    capacity = max(2, (NBR * span_count + peers - 1) // peers + 1)
    block_count = kv_store.shape[0]
    gathered = lax.all_gather(hidden, "store", axis=1, tiled=True)
    values = gathered.astype(jnp.float32)
    normed = (values * lax.rsqrt(jnp.mean(values * values, axis=-1, keepdims=True) + 1e-05)).astype(
        jnp.bfloat16
    )
    queries = jnp.dot(normed, w_query, preferred_element_type=jnp.float32).astype(jnp.bfloat16)
    edge_rows = shifted(queries[: SPAN - 1], "seq", -1)
    attending = jnp.concatenate([queries[SPAN - 1 :], edge_rows], axis=0).reshape(
        span_count, SPAN, width
    )
    request_count = span_count * NBR
    shard_flat = nbr_shard.reshape(request_count)
    block_flat = nbr_block.reshape(request_count)
    same_shard = shard_flat[:, None] == shard_flat[None, :]
    earlier = lax.broadcasted_iota(
        jnp.int32, (request_count, request_count), 0
    ) > lax.broadcasted_iota(jnp.int32, (request_count, request_count), 1)
    rank_ids = jnp.sum((same_shard & earlier).astype(jnp.int32), axis=1)
    slot_ids = shard_flat * capacity + rank_ids
    wanted = (
        jnp.zeros((peers * capacity,), jnp.int32)
        .at[slot_ids]
        .set(block_flat)
        .reshape(peers, capacity)
    )
    kv_local = kv_store.reshape(block_count, NBR_LEN, 2 * width)
    spread = jnp.broadcast_to(attending[:, None], (span_count, NBR, SPAN, width))
    found = kv_local[lax.all_to_all(wanted, "seq", split_axis=0, concat_axis=0, tiled=True)]
    fetched = lax.all_to_all(found, "seq", split_axis=0, concat_axis=0, tiled=True)
    picked = fetched.reshape(peers * capacity, NBR_LEN, 2 * width)[slot_ids]
    picked = picked.reshape(span_count, NBR, NBR_LEN, 2 * width)
    mixed, peaks, totals = partial_attention(spread, picked)
    merged = combine(mixed, peaks, totals, 1)
    attended = jnp.transpose(merged, (0, 2, 1, 3)).reshape(span_count, SPAN, width)
    span_index = lax.axis_index("seq") * span_count + jnp.arange(span_count, dtype=jnp.int32)
    seq_ends = jnp.cumsum(seq_lengths)
    boundary = jnp.any(seq_ends[None, :] == span_index[:, None] + 1, axis=1)
    first_row = jnp.arange(SPAN, dtype=jnp.int32) == 0
    keep_mask = first_row[None, :] | jnp.logical_not(boundary)[:, None]
    masked = (
        jnp.where(keep_mask[..., None], attended, 0.0)
        .astype(jnp.bfloat16)
        .reshape(row_count, width)
    )
    incoming = shifted(masked[row_count - (SPAN - 1) :], "seq", 1)
    att_rows = jnp.concatenate([incoming, masked[: row_count - (SPAN - 1)]], axis=0)
    term = jnp.dot(att_rows, w_out, preferred_element_type=jnp.float32)
    projected = lax.psum_scatter(
        term.astype(jnp.bfloat16), "store", scatter_dimension=1, tiled=True
    ).astype(jnp.float32)
    return (hidden.astype(jnp.float32) + projected).astype(jnp.bfloat16)


def solution(mesh):
    return jax.shard_map(
        on_device,
        mesh=mesh,
        in_specs=(
            P("seq", "store"),
            P("seq", None),
            P("seq", None),
            P(),
            P("seq", None, None, "store"),
            P(None, "store"),
            P("store", None),
        ),
        out_specs=P("seq", "store"),
        check_vma=False,
    )
```

profile of v0, /device:TPU:8, one launch (start us, length us, event | category | flops | bytes accessed | tf_op | source)
XLA Modules:
  0.0 541.5 jit_solution(7445508472138456882)
XLA Ops:
  10.7 11.7 %all-to-all-start = ((s32[32,1,2]{2,1,0:T(1,128)}), s32[32,1,2]{2,1,0:T(1,128)S(1)}, u32[]{:S(2)}, u32[]{:S(2)}) async-start(s32[32,1,2]{2,1,0:T(1,128)} %bitcast.3), calls=%async_computation | async-start | bytes 32768 | tf_op jit(solution)/shard_map/all_to_all | solution.py:79
  22.4 3.2 reshape.169
  25.6 5.3 all-to-all-done
  31.2 7.4 %gather_fusion = bf16[64,128,1024]{2,1,0:T(8,128)(2,1)} fusion(bf16[8,128,1024]{2,1,0:T(8,128)(2,1)S(1)} %reshape.169, s32[1024]{0:T(1024)S(1)} %pad_clamp_fusion.1), kind=kCustom, calls=%fused_computation | custom fusion | bytes 33554688 | tf_op jit(solution)/shard_map/gather | solution.py:79
  38.6 6.5 %all-to-all-start.1 = ((bf16[32,2,128,1024]{3,2,1,0:T(8,128)(2,1)}), bf16[32,2,128,1024]{3,2,1,0:T(8,128)(2,1)}, u32[]{:S(2)}, u32[]{:S(2)}) async-start(bf16[32,2,128,1024]{3,2,1,0:T(8,128)(2,1)} %bitcast.32), calls=%async_computation.1 | async-start | bytes 33554432 | tf_op jit(solution)/shard_map/all_to_all | solution.py:80
  46.6 45.6 %all-gather.2.cloned.1.call-done = bf16[768,4096]{1,0:T(8,128)(2,1)} async-done(((bf16[768,512]{1,0:T(8,128)(2,1)}), bf16[768,4096]{1,0:T(8,128)(2,1)}) %all-gather.2.cloned.1.call-update) | async-done | bytes 6291472 | tf_op jit(solution)/shard_map/all_gather | solution.py:52
  92.3 4.2 fusion
  96.9 5.7 %fusion.11 = bf16[768,512]{1,0:T(8,128)(2,1)S(1)} fusion(bf16[4096,512]{1,0:T(8,128)(2,1)} %param.12, bf16[768,4096]{1,0:T(8,128)(2,1)S(1)} %copy-done.1, f32[768]{0:T(1024)S(1)} %add_rsqrt_fusion), kind=kOutput, calls=%fused_computation.23 | convolution fusion | flops 3231055872 | bytes 11275264 | tf_op jit(solution)/shard_map/dot_general | solution.py:57
  102.6 5.4 collective-permute-start
  108.2 316.4 %collective-permute-done = bf16[63,512]{1,0:T(8,128)(2,1)S(1)} collective-permute-done((bf16[63,512]{1,0:T(8,128)(2,1)S(1)}, bf16[63,512]{1,0:T(8,128)(2,1)S(1)}, u32[]{:S(2)}, u32[]{:S(2)}) %collective-permute-start) | collective-permute-done | bytes 64544 | tf_op jit(solution)/shard_map/ppermute | solution.py:15
  424.8 1.1 copy.61
  425.9 1.9 all-to-all-done.1
  427.8 10.2 %gather_fusion.1 = bf16[24,128,1024]{2,1,0:T(8,128)(2,1)} fusion(bf16[64,128,1024]{2,1,0:T(8,128)(2,1)} %bitcast.6, s32[1024]{0:T(1024)S(1)} %pad_clamp_fusion), kind=kCustom, calls=%fused_computation.1 | custom fusion | bytes 12583008 | tf_op jit(solution)/shard_map/gather | solution.py:81
  438.0 6.2 %fusion.27 = (bf16[12,2,128,512]{3,2,1,0:T(8,128)(2,1)}, bf16[12,2,128,512]{3,2,1,0:T(8,128)(2,1)}) fusion(bf16[12,2,128,1024]{3,2,1,0:T(8,128)(2,1)} %bitcast.33), kind=kLoop, calls=%fused_computation.50 | loop fusion | bytes 12582912 | tf_op jit(solution)/shard_map/slice | solution.py:23
  444.2 3.5 copy.75
  447.7 4.7 copy.76
  452.4 2.2 multiply_reduce_fusion.2
  454.6 2.3 fusion.5
  457.0 2.9 multiply_reduce_fusion
  461.3 1.9 collective-permute-start.1
  463.3 10.7 %collective-permute-done.1 = bf16[63,512]{1,0:T(8,128)(2,1)S(1)} collective-permute-done((bf16[63,512]{1,0:T(8,128)(2,1)S(1)}, bf16[63,512]{1,0:T(8,128)(2,1)S(1)}, u32[]{:S(2)}, u32[]{:S(2)}) %collective-permute-start.1) | collective-permute-done | bytes 64544 | tf_op jit(solution)/shard_map/ppermute | solution.py:15
  474.1 5.3 convolution_convert_fusion
  479.4 53.0 %reduce-scatter.2.cloned.1.call-done = bf16[768,512]{1,0:T(8,128)(2,1)} async-done(((bf16[768,4096]{1,0:T(8,128)(2,1)}), bf16[768,512]{1,0:T(8,128)(2,1)}) %reduce-scatter.2.cloned.1.call-update) | async-done | bytes 786448 | tf_op jit(solution)/shard_map/reduce_scatter | solution.py:99
  532.4 2.2 add_convert_fusion
  (54 shorter events, 8.2 us)
Async XLA Ops:
  10.7 20.2 %all-to-all-start = ((s32[32,1,2]{2,1,0:T(1,128)}), s32[32,1,2]{2,1,0:T(1,128)S(1)}, u32[]{:S(2)}, u32[]{:S(2)}) async-start(s32[32,1,2]{2,1,0:T(1,128)} %bitcast.3), calls=%async_computation | async-start | bytes 32768 | tf_op jit(solution)/shard_map/all_to_all | solution.py:79
  38.6 7.4 %copy-start.3 = (s32[24]{0:T(128)S(1)}, s32[24]{0:T(128)}, u32[]{:S(2)}) copy-start(s32[24]{0:T(128)} %param.10) | copy-start | bytes 292
  38.6 389.2 %all-to-all-start.1 = ((bf16[32,2,128,1024]{3,2,1,0:T(8,128)(2,1)}), bf16[32,2,128,1024]{3,2,1,0:T(8,128)(2,1)}, u32[]{:S(2)}, u32[]{:S(2)}) async-start(bf16[32,2,128,1024]{3,2,1,0:T(8,128)(2,1)} %bitcast.32), calls=%async_computation.1 | async-start | bytes 33554432 | tf_op jit(solution)/shard_map/all_to_all | solution.py:80
  45.1 47.2 %all-gather.2.cloned.1.call-start = ((), (), s32[]{:S(2)}) async-start(), calls=%async_computation.3 | async-start | bytes 7077888 | tf_op jit(solution)/shard_map/all_gather | solution.py:52
  45.8 486.6 %reduce-scatter.2.cloned.1.call-start = ((), (), s32[]{:S(2)}) async-start(), calls=%async_computation.4 | async-start | bytes 7077888 | tf_op jit(solution)/shard_map/reduce_scatter | solution.py:99
  92.3 4.6 copy-start.1
  102.6 322.0 %collective-permute-start = (bf16[63,512]{1,0:T(8,128)(2,1)S(1)}, bf16[63,512]{1,0:T(8,128)(2,1)S(1)}, u32[]{:S(2)}, u32[]{:S(2)}) collective-permute-start(bf16[63,512]{1,0:T(8,128)(2,1)S(1)} %slice.29), channel_id=1, source_target_pairs={{8,0},{16,8},{24,16},{32,24},{40,32},{48,40},{56,48},{64,56},{72,6... | collective-permute-start | bytes 193544 | tf_op jit(solution)/shard_map/ppermute | solution.py:15
  454.6 2.4 copy-start
  459.9 14.2 %copy-start.4 = (bf16[512,4096]{1,0:T(8,128)(2,1)S(1)}, bf16[512,4096]{1,0:T(8,128)(2,1)}, u32[]{:S(2)}) copy-start(bf16[512,4096]{1,0:T(8,128)(2,1)} %param.13) | copy-start | bytes 12582916
  461.3 12.7 %collective-permute-start.1 = (bf16[63,512]{1,0:T(8,128)(2,1)S(1)}, bf16[63,512]{1,0:T(8,128)(2,1)S(1)}, u32[]{:S(2)}, u32[]{:S(2)}) collective-permute-start(bf16[63,512]{1,0:T(8,128)(2,1)S(1)} %slice.32), channel_id=1, source_target_pairs={{0,8},{8,16},{16,24},{24,32},{32,40},{40,48},{48,56},{56,64},{64,7... | collective-permute-start | bytes 193544 | tf_op jit(solution)/shard_map/ppermute | solution.py:15
  479.4 53.0 %copy-start.2 = (bf16[768,512]{1,0:T(8,128)(2,1)S(1)}, bf16[768,512]{1,0:T(8,128)(2,1)}, u32[]{:S(2)}) copy-start(bf16[768,512]{1,0:T(8,128)(2,1)} %param.7) | copy-start | bytes 2359300
Sparse Core Ops, SparseCore 0:
  47.8 44.4 all-gather.1
  479.5 52.8 reduce-scatter.1
where the time goes:
time: 542 us; the launch traced here: 541 us
  waiting for transfers between devices  434 us (80%)
  local copies, waits for them, and re-layouts  41.6 us (8%)
  starting transfers between devices  25.6 us (5%)
  matrix products  16.1 us (3%)
  between operations  13.7 us (3%)
  other arithmetic  10.9 us (2%)
    ppermute x2, waiting for transfers between devices, shifted(): return lax.ppermute(array, axis, pairs)  327 us
    reduce_scatter x1, waiting for transfers between devices, on_device(): lax.psum_scatter(term.astype(jnp.bfloat16), 'store', scatter_dimension=1,...  53 us
    all_gather x1, waiting for transfers between devices, on_device(): gathered = lax.all_gather(hidden, 'store', axis=1, tiled=True)  45.6 us
    all_to_all x1, starting transfers between devices, on_device(): lax.all_to_all(wanted, 'seq', split_axis=0, concat_axis=0, tiled=True)  11.7 us
  transfers between devices with their start and end apart: 6, of which 6 were waited for; matrix products, arithmetic and copies ran while one was open for 3% of the time, Pallas kernels for 0%

commit v1 on v0

v1 whole, which is shorter than its diff:
```python
import functools
import jax
import jax.numpy as jnp
from jax import lax
from jax.experimental import pallas as pl
from jax.experimental.pallas import tpu as pltpu
from jax.sharding import Mesh, PartitionSpec as P

HEAD_DIM = 128
SPAN = 64
NBR = 2
NBR_LEN = 128
HEADS = 4
WIDTH = HEADS * HEAD_DIM
BLK_DEV = 8
NY, NZ, NX, NC = 4, 8, 4, 2
SPANS_DEV = 12
CHUNKS = ((6, 12), (0, 6))
STAT_ROWS = 16
FAR = -1e30
LANES = 128


def ring(array, axis, size, by):
    return lax.ppermute(array, axis, [(i, (i + by) % size) for i in range(size)])


def lane_rows(rows):
    return -(-rows // LANES) * LANES


def load_state(state_ref, out_ref, stat_ref, first, rows):
    out_ref[pl.ds(first, rows), :] = state_ref[pl.ds(0, rows), :]
    wide = lane_rows(rows)
    packed = state_ref[pl.ds(rows, STAT_ROWS), pl.ds(0, wide)].astype(jnp.float32)
    parts = jnp.concatenate([packed, jnp.zeros((LANES - STAT_ROWS, wide), jnp.float32)], axis=0).T
    total = parts + pltpu.roll(parts, LANES - HEADS, 1) + pltpu.roll(parts, LANES - 2 * HEADS, 1)
    stat_ref[pl.ds(first, rows), :] = total[:rows]


def store_stats(stat_ref, out_ref, rows):
    wide = lane_rows(rows)
    lse = stat_ref[pl.ds(0, rows), :]
    if wide != rows:
        lse = jnp.concatenate([lse, jnp.zeros((wide - rows, LANES), jnp.float32)], axis=0)
    high = lse.astype(jnp.bfloat16).astype(jnp.float32)
    rest = lse - high
    middle = rest.astype(jnp.bfloat16).astype(jnp.float32)
    low = rest - middle
    lane = lax.broadcasted_iota(jnp.int32, lse.shape, 1)
    packed = jnp.where(
        lane < HEADS,
        high,
        jnp.where(lane < 2 * HEADS, pltpu.roll(middle, HEADS, 1), pltpu.roll(low, 2 * HEADS, 1)),
    )
    packed = jnp.where(lane < 3 * HEADS, packed, 0.0).T
    out_ref[pl.ds(rows, STAT_ROWS), pl.ds(0, wide)] = packed[:STAT_ROWS].astype(jnp.bfloat16)
    if wide < WIDTH:
        out_ref[pl.ds(rows, STAT_ROWS), pl.ds(wide, WIDTH - wide)] = jnp.zeros(
            (STAT_ROWS, WIDTH - wide), jnp.bfloat16
        )


def merge(old, old_lse, new, new_lse):
    best = jnp.maximum(old_lse, new_lse)
    old_part = jnp.exp(old_lse - best)
    new_part = jnp.exp(new_lse - best)
    both = old_part + new_part
    scale = 1.0 / both
    return old * (old_part * scale) + new * (new_part * scale), best + jnp.log(both)


def attend(q_ref, q_row, block, out_ref, stat_ref, row):
    stats = stat_ref[pl.ds(row, SPAN), :]
    lane = lax.broadcasted_iota(jnp.int32, (SPAN, LANES), 1)
    for head in range(HEADS):
        cols = slice(head * HEAD_DIM, (head + 1) * HEAD_DIM)
        queries = q_ref[pl.ds(q_row, SPAN), cols]
        keys = block[:, cols]
        values = block[:, WIDTH + head * HEAD_DIM : WIDTH + (head + 1) * HEAD_DIM]
        scores = (
            lax.dot_general(
                queries, keys, (((1,), (1,)), ((), ())), preferred_element_type=jnp.float32
            )
            * HEAD_DIM**-0.5
        )
        peaks = jnp.max(scores, axis=-1, keepdims=True)
        weights = jnp.exp(scores - peaks)
        totals = jnp.sum(weights, axis=-1, keepdims=True)
        mixed = jnp.dot(weights.astype(jnp.bfloat16), values, preferred_element_type=jnp.float32)
        old = out_ref[pl.ds(row, SPAN), cols].astype(jnp.float32)
        out, lse = merge(
            old, stats[:, head : head + 1], mixed / totals, peaks + jnp.log(totals)
        )
        out_ref[pl.ds(row, SPAN), cols] = out.astype(jnp.bfloat16)
        stats = jnp.where(lane == head, lse, stats)
    stat_ref[pl.ds(row, SPAN), :] = stats


def kv_copy(kv_ref, buf_ref, sems, block, slot):
    return pltpu.make_async_copy(kv_ref.at[block], buf_ref.at[slot], sems.at[slot])


def start_blocks(ids_ref, base, spans, kv_ref, buf_ref, sems, slot0):
    def one(i, carry):
        block = ids_ref[base + i]

        @pl.when(block >= 0)
        def _():
            kv_copy(kv_ref, buf_ref, sems, block, slot0 + i).start()

        return carry

    lax.fori_loop(0, spans * NBR, one, 0)


def attend_blocks(ids_ref, base, spans, q_ref, kv_ref, buf_ref, sems, slot0, out_ref, stat_ref):
    def one(i, carry):
        block = ids_ref[base + i]

        @pl.when(block >= 0)
        def _():
            kv_copy(kv_ref, buf_ref, sems, block, slot0 + i).wait()
            row = pl.multiple_of((i // NBR) * SPAN, SPAN)
            attend(q_ref, row, buf_ref.at[slot0 + i], out_ref, stat_ref, row)

        return carry

    lax.fori_loop(0, spans * NBR, one, 0)


def relay_kernel(ways, *refs):
    ids_ref, kv_ref = refs[:2]
    refs = refs[2:]
    plan = []
    for base, spans, begin, held in ways:
        q_ref, refs = refs[0], refs[1:]
        state_ref = None
        if held:
            state_ref, refs = refs[0], refs[1:]
        plan.append([base, spans, begin, held, q_ref, state_ref])
    outs, refs = refs[: len(ways)], refs[len(ways) :]
    buf_ref, sems = refs[:2]
    stats = refs[2:]
    slot0 = 0
    for base, spans, *_ in plan:
        start_blocks(ids_ref, base, spans, kv_ref, buf_ref, sems, slot0)
        slot0 += spans * NBR
    slot0 = 0
    for (base, spans, begin, held, q_ref, state_ref), out_ref, stat_ref in zip(plan, outs, stats):
        rows = spans * SPAN
        if held != spans:
            out_ref[pl.ds(0, rows), :] = jnp.zeros((rows, WIDTH), jnp.bfloat16)
            stat_ref[...] = jnp.full((rows, LANES), FAR, jnp.float32)
        if held:
            load_state(state_ref, out_ref, stat_ref, begin * SPAN, held * SPAN)
        attend_blocks(
            ids_ref, base, spans, q_ref, kv_ref, buf_ref, sems, slot0, out_ref, stat_ref
        )
        store_stats(stat_ref, out_ref, rows)
        slot0 += spans * NBR


def final_kernel(base, spans, mask_base, ids_ref, edge_ref, kv_ref, q_ref, fwd_ref, bwd_ref, out_ref, buf_ref, sems, stat_ref, other_ref, other_stat):
    rows = spans * SPAN
    start_blocks(ids_ref, base, spans, kv_ref, buf_ref, sems, 0)
    load_state(fwd_ref, out_ref, stat_ref, 0, rows)
    load_state(bwd_ref, other_ref, other_stat, 0, rows)
    lane = lax.broadcasted_iota(jnp.int32, (rows, LANES), 1)
    stats = stat_ref[...]
    for head in range(HEADS):
        cols = slice(head * HEAD_DIM, (head + 1) * HEAD_DIM)
        out, lse = merge(
            out_ref[:, cols].astype(jnp.float32),
            stat_ref[:, head : head + 1],
            other_ref[:, cols].astype(jnp.float32),
            other_stat[:, head : head + 1],
        )
        out_ref[:, cols] = out.astype(jnp.bfloat16)
        stats = jnp.where(lane == head, lse, stats)
    stat_ref[...] = stats
    attend_blocks(ids_ref, base, spans, q_ref, kv_ref, buf_ref, sems, 0, out_ref, stat_ref)

    def cut(i, carry):
        @pl.when(edge_ref[mask_base + i] > 0)
        def _():
            at = pl.ds(pl.multiple_of(i * SPAN, SPAN), SPAN)
            kept = lax.broadcasted_iota(jnp.int32, (SPAN, WIDTH), 0) == 0
            out_ref[at, :] = jnp.where(kept, out_ref[at, :], jnp.zeros((SPAN, WIDTH), jnp.bfloat16))

        return carry

    lax.fori_loop(0, spans, cut, 0)


SMEM = pl.BlockSpec(memory_space=pltpu.SMEM)
VMEM = pl.BlockSpec(memory_space=pltpu.VMEM)
ANY = pl.BlockSpec(memory_space=pl.ANY)


def cost(pairs, rows):
    return pl.CostEstimate(
        flops=pairs * HEADS * 4 * SPAN * HEAD_DIM * NBR_LEN,
        bytes_accessed=pairs * NBR_LEN * 4 * WIDTH + rows * WIDTH * 8,
        transcendentals=pairs * HEADS * SPAN * NBR_LEN,
    )


def relay(ids, kv, ways):
    specs = [w[:4] for w in ways]
    operands = [ids, kv]
    for base, spans, begin, held, queries, state in ways:
        operands.append(queries)
        if held:
            operands.append(state)
    total = sum(spans for _, spans, _, _ in specs)
    return pl.pallas_call(
        functools.partial(relay_kernel, specs),
        out_shape=[
            jax.ShapeDtypeStruct((spans * SPAN + STAT_ROWS, WIDTH), jnp.bfloat16)
            for _, spans, _, _ in specs
        ],
        in_specs=[SMEM, ANY] + [VMEM] * (len(operands) - 2),
        out_specs=[VMEM] * len(specs),
        scratch_shapes=[
            pltpu.VMEM((total * NBR, NBR_LEN, 2 * WIDTH), jnp.bfloat16),
            pltpu.SemaphoreType.DMA((total * NBR,)),
        ]
        + [pltpu.VMEM((spans * SPAN, LANES), jnp.float32) for _, spans, _, _ in specs],
        compiler_params=pltpu.CompilerParams(vmem_limit_bytes=24 * 1024 * 1024),
        cost_estimate=cost(6, total * SPAN),
    )(*operands)


def finish(ids, edges, kv, base, spans, mask_base, queries, fwd, bwd):
    rows = spans * SPAN
    return pl.pallas_call(
        functools.partial(final_kernel, base, spans, mask_base),
        out_shape=jax.ShapeDtypeStruct((rows, WIDTH), jnp.bfloat16),
        in_specs=[SMEM, SMEM, ANY] + [VMEM] * 3,
        out_specs=VMEM,
        scratch_shapes=[
            pltpu.VMEM((spans * NBR, NBR_LEN, 2 * WIDTH), jnp.bfloat16),
            pltpu.SemaphoreType.DMA((spans * NBR,)),
            pltpu.VMEM((rows, LANES), jnp.float32),
            pltpu.VMEM((rows, WIDTH), jnp.bfloat16),
            pltpu.VMEM((rows, LANES), jnp.float32),
        ],
        compiler_params=pltpu.CompilerParams(vmem_limit_bytes=24 * 1024 * 1024),
        cost_estimate=cost(3, rows),
    )(ids, edges, kv, queries, fwd, bwd)


def on_device(hidden, nbr_shard, nbr_block, seq_lengths, kv_store, w_query, w_out):
    rows = hidden.shape[0]
    my_y, my_z = lax.axis_index("y"), lax.axis_index("z")
    seq_at = my_y * NZ + my_z
    order = [(i, i - 1) for i in range(1, NY * NZ)]
    edge = lax.ppermute(hidden[: SPAN - 1], ("y", "z"), order)
    attending = jnp.concatenate([hidden[SPAN - 1 :], edge], axis=0)

    wanted = nbr_shard * BLK_DEV + nbr_block
    wanted = lax.all_gather(wanted, "z")
    shard, block = wanted // BLK_DEV, wanted % BLK_DEV
    local = jnp.where(
        shard % NZ == my_z, ((shard // NZ - my_y) % NY) * BLK_DEV + block, -1
    ).astype(jnp.int32)
    local = local[(my_z + jnp.arange(NZ)) % NZ].reshape(-1)
    span_index = seq_at * SPANS_DEV + jnp.arange(SPANS_DEV, dtype=jnp.int32)
    boundary = jnp.any(jnp.cumsum(seq_lengths)[None, :] == span_index[:, None] + 1, axis=1)
    boundary = boundary.astype(jnp.int32)

    own = kv_store.reshape(BLK_DEV, NBR_LEN, 2 * WIDTH)
    above = ring(own, "y", NY, -1)
    below = ring(own, "y", NY, 1)
    half = BLK_DEV // 2
    across = jnp.concatenate(
        [ring(above[:half], "y", NY, -1), ring(below[half:], "y", NY, 1)], axis=0
    )
    kv = jnp.concatenate([own, above, across, below], axis=0)

    gathered, queries = [], []
    for first, last in CHUNKS:
        part = lax.all_gather(attending[first * SPAN : last * SPAN], ("x", "core"), axis=1, tiled=True)
        gathered.append(part)
        values = part.astype(jnp.float32)
        scale = lax.rsqrt(jnp.mean(values * values, axis=-1, keepdims=True) + 1e-05)
        product = jnp.dot(part, w_query, preferred_element_type=jnp.float32)
        queries.append((product * scale).astype(jnp.bfloat16))
    w_out, _ = lax.optimization_barrier((w_out, gathered[-1]))
    w_cols = lax.all_to_all(w_out, ("x", "core"), split_axis=1, concat_axis=0, tiled=True)

    outs = []
    for (first, last), mine in zip(CHUNKS, queries):
        spans = last - first
        cut = (spans // 2) * SPAN
        fwd, bwd = [mine], [mine]
        for _ in range(3):
            fwd.append(ring(fwd[-1], "z", NZ, 1))
            bwd.append(ring(bwd[-1], "z", NZ, -1))
        far_top = ring(fwd[3][:cut], "z", NZ, 1)
        far_low = ring(bwd[3][cut:], "z", NZ, -1)

        def base(distance, start=0):
            return ((distance % NZ) * SPANS_DEV + first + start) * NBR

        split = spans // 2
        top, low = relay(
            local,
            kv,
            [
                (base(4), split, 0, 0, far_top, None),
                (base(4, split), spans - split, 0, 0, far_low, None),
            ],
        )
        top, low = ring(top, "z", NZ, 1), ring(low, "z", NZ, -1)
        starts, helds = (0, split), (split, spans - split)
        for s in (3, 2, 1):
            top, low = relay(
                local,
                kv,
                [
                    (base(s), spans, starts[0], helds[0], bwd[s], top),
                    (base(-s), spans, starts[1], helds[1], fwd[s], low),
                ],
            )
            top, low = ring(top, "z", NZ, 1), ring(low, "z", NZ, -1)
            starts, helds = (0, 0), (spans, spans)
        attended = finish(local, boundary, kv, base(0), spans, first, mine, top, low)
        whole = lax.all_gather(attended, ("x", "core"), axis=1, tiled=True)
        projected = jnp.dot(whole, w_cols, preferred_element_type=jnp.float32)
        residual = attending[first * SPAN : last * SPAN].astype(jnp.float32)
        outs.append((residual + projected).astype(jnp.bfloat16))

    result = jnp.concatenate([o for _, o in sorted(zip([c[0] for c in CHUNKS], outs), key=lambda p: p[0])], axis=0)
    order = [(i, i + 1) for i in range(NY * NZ - 1)]
    head = lax.ppermute(result[rows - (SPAN - 1) :], ("y", "z"), order)
    head = jnp.where(seq_at == 0, hidden[: SPAN - 1], head)
    return jnp.concatenate([head, result[: rows - (SPAN - 1)]], axis=0)


def solution(mesh):
    fine = Mesh(mesh.devices.reshape(NY, NZ, NX, NC), ("y", "z", "x", "core"))
    seq, store = ("y", "z"), ("x", "core")
    return jax.shard_map(
        on_device,
        mesh=fine,
        in_specs=(
            P(seq, store),
            P(seq, None),
            P(seq, None),
            P(),
            P(seq, None, None, store),
            P(None, store),
            P(store, None),
        ),
        out_specs=P(seq, store),
        check_vma=False,
    )
```

time: 542 us -> 446 us (0.82)
  waiting for transfers between devices: 434 us -> 187 us
  Pallas kernels: 0 us -> 76.2 us
  starting transfers between devices: 25.6 us -> 82.1 us
  blocking collectives: 0 us -> 17.7 us
  local copies, waits for them, and re-layouts: 41.6 us -> 36 us
    ppermute x2 -> x38, waiting for transfers between devices: 327 us -> 101 us  [the longest x36 99.1 us: ring(): lax.ppermute(array, axis, [(i, (i + by) % size) for i in range(size)])]
    pallas_call x0 -> x10, Pallas kernels: none -> 76.2 us  [the longest x8 62.4 us: relay(): pl.pallas_call(functools.partial(relay_kernel, specs), out_shape=[jax.Sha...]
    ppermute x2 -> x38, starting transfers between devices: 7.31 us -> 77.1 us  [the longest x36 67.6 us: ring(): lax.ppermute(array, axis, [(i, (i + by) % size) for i in range(size)])]
    all_to_all x2 -> x1, waiting for transfers between devices: 7.17 us -> 62.3 us  [on_device(): lax.all_to_all(w_out, ('x', 'core'), split_axis=1, concat_axis=0, tiled=T...]
    reduce_scatter x1 -> x0, waiting for transfers between devices: 53 us -> none  [on_device(): lax.psum_scatter(term.astype(jnp.bfloat16), 'store', scatter_dimension=1,...]
    all_gather x1 -> x4, waiting for transfers between devices: 45.6 us -> 23.4 us  [the longest x2 23.4 us: on_device(): lax.all_gather(attending[first * SPAN:last * SPAN], ('x', 'core'), axis=1...]
    all_gather x0 -> x1, blocking collectives: none -> 17.7 us  [on_device(): wanted = lax.all_gather(wanted, 'z')]
    gather x2, local copies, waits for them, and re-layouts: 17.6 us -> 0.72 us  [on_device(): local = local[(my_z + jnp.arange(NZ)) % NZ].reshape(-1)]
  transfers between devices with their start and end apart: 6 -> 43, of which waited for: 6 -> 20; matrix products, arithmetic and copies ran while one was open for 3% -> 13% of each run, Pallas kernels for 0% -> 17%
where the time goes in v1:
time: 446 us; the launch traced here: 440 us
  waiting for transfers between devices  187 us (42%)
  starting transfers between devices  82.1 us (18%)
  Pallas kernels  76.2 us (17%)
  local copies, waits for them, and re-layouts  36 us (8%)
  matrix products  19.9 us (4%)
  blocking collectives  17.7 us (4%)
  between operations  14.1 us (3%)
  other arithmetic  7.49 us (2%)
    ppermute x36, waiting for transfers between devices, ring(): lax.ppermute(array, axis, [(i, (i + by) % size) for i in range(size)])  99.1 us
    ppermute x36, starting transfers between devices, ring(): lax.ppermute(array, axis, [(i, (i + by) % size) for i in range(size)])  67.6 us
    pallas_call x8, Pallas kernels, relay(): pl.pallas_call(functools.partial(relay_kernel, specs), out_shape=[jax.Sha...  62.4 us
    all_to_all x1, waiting for transfers between devices, on_device(): lax.all_to_all(w_out, ('x', 'core'), split_axis=1, concat_axis=0, tiled=T...  62.3 us
    all_gather x2, waiting for transfers between devices, on_device(): lax.all_gather(attending[first * SPAN:last * SPAN], ('x', 'core'), axis=1...  23.4 us
    all_gather x1, blocking collectives, on_device(): wanted = lax.all_gather(wanted, 'z')  17.7 us
    pallas_call x2, Pallas kernels, finish(): pl.pallas_call(functools.partial(final_kernel, base, spans, mask_base), o...  13.8 us
    dot_general x2, matrix products, on_device(): product = jnp.dot(part, w_query, preferred_element_type=jnp.float32)  10 us
  transfers between devices with their start and end apart: 43, of which 20 were waited for; matrix products, arithmetic and copies ran while one was open for 13% of the time, Pallas kernels for 17%

profile of v1, /device:TPU:8, one launch (start us, length us, event | category | flops | bytes accessed | tf_op | source)
XLA Modules:
  0.0 440.2 jit_solution(12904022189093717943)
XLA Ops:
  7.4 7.6 %collective-permute-start = (bf16[63,512]{1,0:T(8,128)(2,1)S(1)}, bf16[63,512]{1,0:T(8,128)(2,1)S(1)}, u32[]{:S(2)}, u32[]{:S(2)}) collective-permute-start(bf16[63,512]{1,0:T(8,128)(2,1)S(1)} %slice.40), channel_id=1, source_target_pairs={{8,0},{16,8},{24,16},{32,24},{40,32},{48,40},{56,48},{64,56},{72,6... | collective-permute-start | bytes 193544 | tf_op jit(solution)/shard_map/ppermute | solution.py:259
  25.1 23.4 %all-gather.7.cloned.1.call-done = bf16[384,4096]{1,0:T(8,128)(2,1)} async-done(((bf16[384,512]{1,0:T(8,128)(2,1)}), bf16[384,4096]{1,0:T(8,128)(2,1)}) %all-gather.7.cloned.1.call-update) | async-done | bytes 3145744 | tf_op jit(solution)/shard_map/all_gather | solution.py:284
  59.5 10.2 %collective-permute-done.1 = bf16[8,128,1024]{2,1,0:T(8,128)(2,1)} collective-permute-done((bf16[8,128,1024]{2,1,0:T(8,128)(2,1)S(1)}, bf16[8,128,1024]{2,1,0:T(8,128)(2,1)}, u32[]{:S(2)}, u32[]{:S(2)}) %collective-permute-start.1) | collective-permute-done | bytes 2097184 | tf_op jit(solution)/shard_map/ppermute | solution.py:25
  76.3 17.7 %all-gather.1 = s32[8,12,2]{1,2,0:T(2,128)S(1)} all-gather(s32[1,12,2]{1,2,0:T(2,128)S(1)} %add_bitcast_fusion), channel_id=2, replica_groups=mesh['y'=4,'z'=8,'x'=4,'core'=2] {'z'}, dimensions={0}, use_global_device_ids=true | all-gather | bytes 864 | tf_op jit(solution)/shard_map/all_gather | solution.py:263
  98.2 8.4 %collective-permute-done.9.refs_4_ = bf16[384,512]{1,0:T(8,128)(2,1)S(1)} collective-permute-done((bf16[384,512]{1,0:T(8,128)(2,1)S(1)}, bf16[384,512]{1,0:T(8,128)(2,1)S(1)}, u32[]{:S(2)}, u32[]{:S(2)}) %collective-permute-start.9) | collective-permute-done | bytes 393248 | tf_op jit(solution)/shard_map/ppermute | solution.py:25
  137.5 10.1 %shard_map.74 = (bf16[400,512]{1,0:T(8,128)(2,1)S(1)}, bf16[400,512]{1,0:T(8,128)(2,1)S(1)}) custom-call(s32[192]{0:T(256)S(1)} %reshape.104.refs_0_.ids_ref, bf16[32,128,1024]{2,1,0:T(8,128)(2,1)S(1)} %constant_dynamic-update-slice_fusion.refs_1_.kv_ref, bf16[384,512]{1,0:T(8,128)(2,1)S(1)} %collective-permute-done.7.refs_2_, ...), custom_call_target="tpu_custom_call" | custom-call | flops 100663296 | bytes 4718592 | tf_op jit(solution)/shard_map/pallas_call | solution.py:217
  156.9 7.5 %shard_map.75 = (bf16[400,512]{1,0:T(8,128)(2,1)S(1)}, bf16[400,512]{1,0:T(8,128)(2,1)S(1)}) custom-call(s32[192]{0:T(256)S(1)} %reshape.104.refs_0_.ids_ref, bf16[32,128,1024]{2,1,0:T(8,128)(2,1)S(1)} %constant_dynamic-update-slice_fusion.refs_1_.kv_ref, bf16[384,512]{1,0:T(8,128)(2,1)S(1)} %collective-permute-done.6.refs_2_, ...), custom_call_target="tpu_custom_call" | custom-call | flops 100663296 | bytes 4718592 | tf_op jit(solution)/shard_map/pallas_call | solution.py:217
  167.7 5.9 %collective-permute-done.17.refs_3_ = bf16[400,512]{1,0:T(8,128)(2,1)S(1)} collective-permute-done((bf16[400,512]{1,0:T(8,128)(2,1)S(1)}, bf16[400,512]{1,0:T(8,128)(2,1)S(1)}, u32[]{:S(2)}, u32[]{:S(2)}) %collective-permute-start.17) | collective-permute-done | bytes 409632 | tf_op jit(solution)/shard_map/ppermute | solution.py:25
  173.7 10.2 %shard_map.76 = (bf16[400,512]{1,0:T(8,128)(2,1)S(1)}, bf16[400,512]{1,0:T(8,128)(2,1)S(1)}) custom-call(s32[192]{0:T(256)S(1)} %reshape.104.refs_0_.ids_ref, bf16[32,128,1024]{2,1,0:T(8,128)(2,1)S(1)} %constant_dynamic-update-slice_fusion.refs_1_.kv_ref, bf16[384,512]{1,0:T(8,128)(2,1)S(1)} %collective-permute-done.5.refs_2_, ...), custom_call_target="tpu_custom_call" | custom-call | flops 100663296 | bytes 4718592 | tf_op jit(solution)/shard_map/pallas_call | solution.py:217
  183.9 8.9 %collective-permute-start.19 = (bf16[400,512]{1,0:T(8,128)(2,1)S(1)}, bf16[400,512]{1,0:T(8,128)(2,1)S(1)}, u32[]{:S(2)}, u32[]{:S(2)}) collective-permute-start(bf16[400,512]{1,0:T(8,128)(2,1)S(1)} %get-tuple-element.28), channel_id=1, source_target_pairs={{0,8},{8,16},{16,24},{24,32},{32,40},{40,48},{48,56},{56,0},{1,9},... | collective-permute-start | bytes 1228808 | tf_op jit(solution)/shard_map/ppermute | solution.py:25
  205.3 6.9 %shard_map.77 = bf16[384,512]{1,0:T(8,128)(2,1)} custom-call(s32[192]{0:T(256)S(1)} %reshape.104.refs_0_.ids_ref, s32[12]{0:T(128)S(1)} %convert_element_type.28.edge_ref, bf16[32,128,1024]{2,1,0:T(8,128)(2,1)S(1)} %copy-done.1, bf16[384,512]{1,0:T(8,128)(2,1)S(1)} %fusion.1.q_ref, bf16[400,512]{1,0:T(8,128)(2,1)S(1)} %collective-permute-done.19.fwd_ref, ...), custom_call_target="tpu_custom_call" | custom-call | flops 50331648 | bytes 2359296 | tf_op jit(solution)/shard_map/pallas_call | solution.py:237
  223.3 9.0 %collective-permute-done.25.refs_4_ = bf16[384,512]{1,0:T(8,128)(2,1)S(1)} collective-permute-done((bf16[384,512]{1,0:T(8,128)(2,1)S(1)}, bf16[384,512]{1,0:T(8,128)(2,1)S(1)}, u32[]{:S(2)}, u32[]{:S(2)}) %collective-permute-start.25) | collective-permute-done | bytes 393248 | tf_op jit(solution)/shard_map/ppermute | solution.py:25
  235.9 7.5 %collective-permute-done.26.refs_4_ = bf16[384,512]{1,0:T(8,128)(2,1)S(1)} collective-permute-done((bf16[384,512]{1,0:T(8,128)(2,1)S(1)}, bf16[384,512]{1,0:T(8,128)(2,1)S(1)}, u32[]{:S(2)}, u32[]{:S(2)}) %collective-permute-start.26) | collective-permute-done | bytes 393248 | tf_op jit(solution)/shard_map/ppermute | solution.py:25
  246.9 7.7 %collective-permute-done.27.refs_4_ = bf16[384,512]{1,0:T(8,128)(2,1)S(1)} collective-permute-done((bf16[384,512]{1,0:T(8,128)(2,1)S(1)}, bf16[384,512]{1,0:T(8,128)(2,1)S(1)}, u32[]{:S(2)}, u32[]{:S(2)}) %collective-permute-start.27) | collective-permute-done | bytes 393248 | tf_op jit(solution)/shard_map/ppermute | solution.py:25
  274.0 8.8 %shard_map.79 = (bf16[400,512]{1,0:T(8,128)(2,1)S(1)}, bf16[400,512]{1,0:T(8,128)(2,1)S(1)}) custom-call(s32[192]{0:T(256)S(1)} %reshape.104.refs_0_.ids_ref, bf16[32,128,1024]{2,1,0:T(8,128)(2,1)S(1)} %bitcast.17, bf16[384,512]{1,0:T(8,128)(2,1)S(1)} %collective-permute-done.24.refs_2_, bf16[208,512]{1,0:T(8,128)(2,1)S(1)} %collective-permute-done.30.refs_3_, ...), custom_call_target="tpu_custom_call" | custom-call | flops 100663296 | bytes 4718592 | tf_op jit(solution)/shard_map/pallas_call | solution.py:217
  286.1 8.1 %collective-permute-done.32.refs_3_ = bf16[400,512]{1,0:T(8,128)(2,1)S(1)} collective-permute-done((bf16[400,512]{1,0:T(8,128)(2,1)S(1)}, bf16[400,512]{1,0:T(8,128)(2,1)S(1)}, u32[]{:S(2)}, u32[]{:S(2)}) %collective-permute-start.32) | collective-permute-done | bytes 409632 | tf_op jit(solution)/shard_map/ppermute | solution.py:25
  294.2 8.9 %shard_map.80 = (bf16[400,512]{1,0:T(8,128)(2,1)S(1)}, bf16[400,512]{1,0:T(8,128)(2,1)S(1)}) custom-call(s32[192]{0:T(256)S(1)} %reshape.104.refs_0_.ids_ref, bf16[32,128,1024]{2,1,0:T(8,128)(2,1)S(1)} %bitcast.17, bf16[384,512]{1,0:T(8,128)(2,1)S(1)} %collective-permute-done.23.refs_2_, bf16[400,512]{1,0:T(8,128)(2,1)S(1)} %collective-permute-done.32.refs_3_, ...), custom_call_target="tpu_custom_call" | custom-call | flops 100663296 | bytes 4718592 | tf_op jit(solution)/shard_map/pallas_call | solution.py:217
  306.4 7.2 %collective-permute-done.34.refs_3_ = bf16[400,512]{1,0:T(8,128)(2,1)S(1)} collective-permute-done((bf16[400,512]{1,0:T(8,128)(2,1)S(1)}, bf16[400,512]{1,0:T(8,128)(2,1)S(1)}, u32[]{:S(2)}, u32[]{:S(2)}) %collective-permute-start.34) | collective-permute-done | bytes 409632 | tf_op jit(solution)/shard_map/ppermute | solution.py:25
  313.6 8.9 %shard_map.81 = (bf16[400,512]{1,0:T(8,128)(2,1)S(1)}, bf16[400,512]{1,0:T(8,128)(2,1)S(1)}) custom-call(s32[192]{0:T(256)S(1)} %reshape.104.refs_0_.ids_ref, bf16[32,128,1024]{2,1,0:T(8,128)(2,1)S(1)} %bitcast.17, bf16[384,512]{1,0:T(8,128)(2,1)S(1)} %collective-permute-done.22.refs_2_, bf16[400,512]{1,0:T(8,128)(2,1)S(1)} %collective-permute-done.34.refs_3_, ...), custom_call_target="tpu_custom_call" | custom-call | flops 100663296 | bytes 4718592 | tf_op jit(solution)/shard_map/pallas_call | solution.py:217
  325.8 5.9 %collective-permute-done.36.fwd_ref = bf16[400,512]{1,0:T(8,128)(2,1)S(1)} collective-permute-done((bf16[400,512]{1,0:T(8,128)(2,1)S(1)}, bf16[400,512]{1,0:T(8,128)(2,1)S(1)}, u32[]{:S(2)}, u32[]{:S(2)}) %collective-permute-start.36) | collective-permute-done | bytes 409632 | tf_op jit(solution)/shard_map/ppermute | solution.py:25
  331.8 6.9 %shard_map.82 = bf16[384,512]{1,0:T(8,128)(2,1)} custom-call(s32[192]{0:T(256)S(1)} %reshape.104.refs_0_.ids_ref, s32[12]{0:T(128)S(1)} %convert_element_type.28.edge_ref, bf16[32,128,1024]{2,1,0:T(8,128)(2,1)S(1)} %bitcast.17, bf16[384,512]{1,0:T(8,128)(2,1)S(1)} %fusion.2.q_ref, bf16[400,512]{1,0:T(8,128)(2,1)S(1)} %collective-permute-done.36.fwd_ref, ...), custom_call_target="tpu_custom_call" | custom-call | flops 50331648 | bytes 2359296 | tf_op jit(solution)/shard_map/pallas_call | solution.py:237
  338.7 6.5 %copy.21 = bf16[512,4096]{0,1:T(8,128)(2,1)} copy(bf16[512,4096]{1,0:T(8,128)(2,1)} %param.13) | data formatting | bytes 8388608 | tf_op jit(solution)/shard_map/optimization_barrier | solution.py:290
  350.0 62.3 %all-to-all-done = bf16[512,8,512]{0,2,1:T(8,128)(2,1)} async-done(((bf16[512,8,512]{0,2,1:T(8,128)(2,1)}), bf16[512,8,512]{0,2,1:T(8,128)(2,1)}, u32[]{:S(2)}, u32[]{:S(2)}) %all-to-all-start) | async-done | bytes 4194336 | tf_op jit(solution)/shard_map/all_to_all | solution.py:291
  412.3 6.5 %copy.22 = bf16[8,512,512]{2,1,0:T(8,128)(2,1)} copy(bf16[8,512,512]{1,2,0:T(8,128)(2,1)} %bitcast.4) | data formatting | bytes 8388608 | tf_op jit(solution)/shard_map/all_to_all | solution.py:291
  (140 shorter events, 155.0 us)
Async XLA Ops:
  6.5 41.9 %all-gather.7.cloned.1.call-start = ((), (), s32[]{:S(2)}) async-start(), calls=%async_computation.1 | async-start | bytes 3538944 | tf_op jit(solution)/shard_map/all_gather | solution.py:284
  17.7 194.6 %all-gather.11.cloned.1.call-start = ((), (), s32[]{:S(2)}) async-start(), calls=%async_computation.3 | async-start | bytes 3538944 | tf_op jit(solution)/shard_map/all_gather | solution.py:284
  19.7 399.2 %all-gather.9.cloned.1.call-start = ((), (), s32[]{:S(2)}) async-start(), calls=%async_computation.2 | async-start | bytes 3538944 | tf_op jit(solution)/shard_map/all_gather | solution.py:330
  23.0 46.7 %collective-permute-start.1 = (bf16[8,128,1024]{2,1,0:T(8,128)(2,1)S(1)}, bf16[8,128,1024]{2,1,0:T(8,128)(2,1)}, u32[]{:S(2)}, u32[]{:S(2)}) collective-permute-start(bf16[8,128,1024]{2,1,0:T(8,128)(2,1)S(1)} %reshape.107), channel_id=1, source_target_pairs={{0,192},{64,0},{128,64},{192,128},{1,193},{65,1},{129,65},{193,129... | collective-permute-start | bytes 6291464 | tf_op jit(solution)/shard_map/ppermute | solution.py:25
  23.1 50.1 %collective-permute-start.3 = (bf16[8,128,1024]{2,1,0:T(8,128)(2,1)S(1)}, bf16[8,128,1024]{2,1,0:T(8,128)(2,1)}, u32[]{:S(2)}, u32[]{:S(2)}) collective-permute-start(bf16[8,128,1024]{2,1,0:T(8,128)(2,1)S(1)} %reshape.107), channel_id=1, source_target_pairs={{0,64},{64,128},{128,192},{192,0},{1,65},{65,129},{129,193},{193,1... | collective-permute-start | bytes 6291464 | tf_op jit(solution)/shard_map/ppermute | solution.py:25
  56.0 38.0 %collective-permute-start.8 = (bf16[384,512]{1,0:T(8,128)(2,1)S(1)}, bf16[384,512]{1,0:T(8,128)(2,1)S(1)}, u32[]{:S(2)}, u32[]{:S(2)}) collective-permute-start(bf16[384,512]{1,0:T(8,128)(2,1)S(1)} %fusion.1.q_ref), channel_id=1, source_target_pairs={{0,8},{8,16},{16,24},{24,32},{32,40},{40,48},{48,56},{56,0},{1,9},... | collective-permute-start | bytes 1179656 | tf_op jit(solution)/shard_map/ppermute | solution.py:25
  57.6 36.4 %collective-permute-start.5 = (bf16[384,512]{1,0:T(8,128)(2,1)S(1)}, bf16[384,512]{1,0:T(8,128)(2,1)S(1)}, u32[]{:S(2)}, u32[]{:S(2)}) collective-permute-start(bf16[384,512]{1,0:T(8,128)(2,1)S(1)} %fusion.1.q_ref), channel_id=1, source_target_pairs={{0,56},{8,0},{16,8},{24,16},{32,24},{40,32},{48,40},{56,48},{1,57}... | collective-permute-start | bytes 1179656 | tf_op jit(solution)/shard_map/ppermute | solution.py:25
  72.0 41.7 %collective-permute-start.2 = (bf16[4,128,1024]{2,1,0:T(8,128)(2,1)}, bf16[4,128,1024]{2,1,0:T(8,128)(2,1)}, u32[]{:S(2)}, u32[]{:S(2)}) collective-permute-start(bf16[4,128,1024]{2,1,0:T(8,128)(2,1)} %slice.54), channel_id=1, source_target_pairs={{0,192},{64,0},{128,64},{192,128},{1,193},{65,1},{129,65},{193,129... | collective-permute-start | bytes 3145736 | tf_op jit(solution)/shard_map/ppermute | solution.py:25
  75.5 45.7 %collective-permute-start.4 = (bf16[4,128,1024]{2,1,0:T(8,128)(2,1)}, bf16[4,128,1024]{2,1,0:T(8,128)(2,1)S(1)}, u32[]{:S(2)}, u32[]{:S(2)}) collective-permute-start(bf16[4,128,1024]{2,1,0:T(8,128)(2,1)} %slice.55), channel_id=1, source_target_pairs={{0,64},{64,128},{128,192},{192,0},{1,65},{65,129},{129,193},{193,1... | collective-permute-start | bytes 3145736 | tf_op jit(solution)/shard_map/ppermute | solution.py:25
  94.0 12.6 %collective-permute-start.9 = (bf16[384,512]{1,0:T(8,128)(2,1)S(1)}, bf16[384,512]{1,0:T(8,128)(2,1)S(1)}, u32[]{:S(2)}, u32[]{:S(2)}) collective-permute-start(bf16[384,512]{1,0:T(8,128)(2,1)S(1)} %collective-permute-done.8.refs_4_), channel_id=1, source_target_pairs={{0,8},{8,16},{16,24},{24,32},{32,40},{40,48},{48,56},{56,0},{1,9},... | collective-permute-start | bytes 1179656 | tf_op jit(solution)/shard_map/ppermute | solution.py:25
  94.0 12.6 %collective-permute-start.6 = (bf16[384,512]{1,0:T(8,128)(2,1)S(1)}, bf16[384,512]{1,0:T(8,128)(2,1)S(1)}, u32[]{:S(2)}, u32[]{:S(2)}) collective-permute-start(bf16[384,512]{1,0:T(8,128)(2,1)S(1)} %collective-permute-done.5.refs_2_), channel_id=1, source_target_pairs={{0,56},{8,0},{16,8},{24,16},{32,24},{40,32},{48,40},{56,48},{1,57}... | collective-permute-start | bytes 1179656 | tf_op jit(solution)/shard_map/ppermute | solution.py:25
  106.6 10.9 %collective-permute-start.10 = (bf16[384,512]{1,0:T(8,128)(2,1)S(1)}, bf16[384,512]{1,0:T(8,128)(2,1)S(1)}, u32[]{:S(2)}, u32[]{:S(2)}) collective-permute-start(bf16[384,512]{1,0:T(8,128)(2,1)S(1)} %collective-permute-done.9.refs_4_), channel_id=1, source_target_pairs={{0,8},{8,16},{16,24},{24,32},{32,40},{40,48},{48,56},{56,0},{1,9},... | collective-permute-start | bytes 1179656 | tf_op jit(solution)/shard_map/ppermute | solution.py:25
  106.6 11.3 %collective-permute-start.7 = (bf16[384,512]{1,0:T(8,128)(2,1)S(1)}, bf16[384,512]{1,0:T(8,128)(2,1)S(1)}, u32[]{:S(2)}, u32[]{:S(2)}) collective-permute-start(bf16[384,512]{1,0:T(8,128)(2,1)S(1)} %collective-permute-done.6.refs_2_), channel_id=1, source_target_pairs={{0,56},{8,0},{16,8},{24,16},{32,24},{40,32},{48,40},{56,48},{1,57}... | collective-permute-start | bytes 1179656 | tf_op jit(solution)/shard_map/ppermute | solution.py:25
  183.9 18.1 %collective-permute-start.19 = (bf16[400,512]{1,0:T(8,128)(2,1)S(1)}, bf16[400,512]{1,0:T(8,128)(2,1)S(1)}, u32[]{:S(2)}, u32[]{:S(2)}) collective-permute-start(bf16[400,512]{1,0:T(8,128)(2,1)S(1)} %get-tuple-element.28), channel_id=1, source_target_pairs={{0,8},{8,16},{16,24},{24,32},{32,40},{40,48},{48,56},{56,0},{1,9},... | collective-permute-start | bytes 1228808 | tf_op jit(solution)/shard_map/ppermute | solution.py:25
  212.3 213.5 %all-gather.13.cloned.1.call-start = ((), (), s32[]{:S(2)}) async-start(), calls=%async_computation.4 | async-start | bytes 3538944 | tf_op jit(solution)/shard_map/all_gather | solution.py:330
  220.0 12.3 %collective-permute-start.25 = (bf16[384,512]{1,0:T(8,128)(2,1)S(1)}, bf16[384,512]{1,0:T(8,128)(2,1)S(1)}, u32[]{:S(2)}, u32[]{:S(2)}) collective-permute-start(bf16[384,512]{1,0:T(8,128)(2,1)S(1)} %fusion.2.q_ref), channel_id=1, source_target_pairs={{0,8},{8,16},{16,24},{24,32},{32,40},{40,48},{48,56},{56,0},{1,9},... | collective-permute-start | bytes 1179656 | tf_op jit(solution)/shard_map/ppermute | solution.py:25
  220.1 12.2 %collective-permute-start.22 = (bf16[384,512]{1,0:T(8,128)(2,1)S(1)}, bf16[384,512]{1,0:T(8,128)(2,1)S(1)}, u32[]{:S(2)}, u32[]{:S(2)}) collective-permute-start(bf16[384,512]{1,0:T(8,128)(2,1)S(1)} %fusion.2.q_ref), channel_id=1, source_target_pairs={{0,56},{8,0},{16,8},{24,16},{32,24},{40,32},{48,40},{56,48},{1,57}... | collective-permute-start | bytes 1179656 | tf_op jit(solution)/shard_map/ppermute | solution.py:25
  232.3 11.1 %collective-permute-start.26 = (bf16[384,512]{1,0:T(8,128)(2,1)S(1)}, bf16[384,512]{1,0:T(8,128)(2,1)S(1)}, u32[]{:S(2)}, u32[]{:S(2)}) collective-permute-start(bf16[384,512]{1,0:T(8,128)(2,1)S(1)} %collective-permute-done.25.refs_4_), channel_id=1, source_target_pairs={{0,8},{8,16},{16,24},{24,32},{32,40},{40,48},{48,56},{56,0},{1,9},... | collective-permute-start | bytes 1179656 | tf_op jit(solution)/shard_map/ppermute | solution.py:25
  232.3 11.1 %collective-permute-start.23 = (bf16[384,512]{1,0:T(8,128)(2,1)S(1)}, bf16[384,512]{1,0:T(8,128)(2,1)S(1)}, u32[]{:S(2)}, u32[]{:S(2)}) collective-permute-start(bf16[384,512]{1,0:T(8,128)(2,1)S(1)} %collective-permute-done.22.refs_2_), channel_id=1, source_target_pairs={{0,56},{8,0},{16,8},{24,16},{32,24},{40,32},{48,40},{56,48},{1,57}... | collective-permute-start | bytes 1179656 | tf_op jit(solution)/shard_map/ppermute | solution.py:25
  243.4 11.3 %collective-permute-start.27 = (bf16[384,512]{1,0:T(8,128)(2,1)S(1)}, bf16[384,512]{1,0:T(8,128)(2,1)S(1)}, u32[]{:S(2)}, u32[]{:S(2)}) collective-permute-start(bf16[384,512]{1,0:T(8,128)(2,1)S(1)} %collective-permute-done.26.refs_4_), channel_id=1, source_target_pairs={{0,8},{8,16},{16,24},{24,32},{32,40},{40,48},{48,56},{56,0},{1,9},... | collective-permute-start | bytes 1179656 | tf_op jit(solution)/shard_map/ppermute | solution.py:25
  243.4 11.4 %collective-permute-start.24 = (bf16[384,512]{1,0:T(8,128)(2,1)S(1)}, bf16[384,512]{1,0:T(8,128)(2,1)S(1)}, u32[]{:S(2)}, u32[]{:S(2)}) collective-permute-start(bf16[384,512]{1,0:T(8,128)(2,1)S(1)} %collective-permute-done.23.refs_2_), channel_id=1, source_target_pairs={{0,56},{8,0},{16,8},{24,16},{32,24},{40,32},{48,40},{56,48},{1,57}... | collective-permute-start | bytes 1179656 | tf_op jit(solution)/shard_map/ppermute | solution.py:25
  282.8 11.4 %collective-permute-start.32 = (bf16[400,512]{1,0:T(8,128)(2,1)S(1)}, bf16[400,512]{1,0:T(8,128)(2,1)S(1)}, u32[]{:S(2)}, u32[]{:S(2)}) collective-permute-start(bf16[400,512]{1,0:T(8,128)(2,1)S(1)} %get-tuple-element.33), channel_id=1, source_target_pairs={{0,8},{8,16},{16,24},{24,32},{32,40},{40,48},{48,56},{56,0},{1,9},... | collective-permute-start | bytes 1228808 | tf_op jit(solution)/shard_map/ppermute | solution.py:25
  283.3 11.0 %collective-permute-start.33 = (bf16[400,512]{1,0:T(8,128)(2,1)S(1)}, bf16[400,512]{1,0:T(8,128)(2,1)S(1)}, u32[]{:S(2)}, u32[]{:S(2)}) collective-permute-start(bf16[400,512]{1,0:T(8,128)(2,1)S(1)} %get-tuple-element.34), channel_id=1, source_target_pairs={{0,56},{8,0},{16,8},{24,16},{32,24},{40,32},{48,40},{56,48},{1,57}... | collective-permute-start | bytes 1228808 | tf_op jit(solution)/shard_map/ppermute | solution.py:25
  345.2 67.1 %all-to-all-start = ((bf16[512,8,512]{0,2,1:T(8,128)(2,1)}), bf16[512,8,512]{0,2,1:T(8,128)(2,1)}, u32[]{:S(2)}, u32[]{:S(2)}) async-start(bf16[512,8,512]{0,2,1:T(8,128)(2,1)} %bitcast.18), calls=%async_computation | async-start | bytes 8388608 | tf_op jit(solution)/shard_map/all_to_all | solution.py:291
  (29 other events, 430.8 us)
Sparse Core Ops, SparseCore 0:
  17.8 30.5 all-gather.6
  50.3 30.3 all-gather.10
  212.4 29.0 all-gather.8
  338.8 49.2 all-gather.12
